TPU v7x, 128 devices: a whole 4x4x4 slice. The times are simulated.
128 devices in a mesh: ab: 32 (over x, z, y_lo), cd: 4 (over y_hi, core).
Axes of the slice: x: 4, y: 4 (y_hi: 2, y_lo: 2; y = y_hi * 2 + y_lo), z: 4, core: 2. Of those that a mesh axis runs over, the one named last changes fastest.
Arguments:
- integrals: bfloat16 [96, 96, 128, 512], P('ab', None, None, 'cd'), may hold values from -0.0234375 to 0.0234375
- amplitudes: bfloat16 [16, 512, 512], P(None, 'ab', 'cd'), may hold values from -6 to 6
- block_sizes: int32 [4], replicated, may hold values from 1 to 128, 500 in all
Outputs:
- symmetric_residual: float32 [16, 96, 96], P(None, 'ab')
Inputs may be any that keep to these rules, and one draw needn't show every extreme that they name: `block_sizes`: the sizes sum to 500 and the largest is exactly 128.
All inputs are finite; a program needn't handle non-finite values.
Results may differ from a plain program's by a relative error of at most 0.0003.
Values may be sent and summed in bfloat16 or wider, within the bound.
A program may use at most 64 MiB of HBM per device.

v0:
```python
import jax
import jax.numpy as jnp
from jax import lax
from jax.sharding import PartitionSpec as P

IRREPS = 4
BLK = 128


def occupied_slots(block_sizes, first_slot, count):
    slot_ids = first_slot + jnp.arange(count, dtype=jnp.int32)
    irrep_ids = slot_ids // BLK
    owners = jnp.arange(IRREPS, dtype=jnp.int32)
    limits = jnp.sum(
        jnp.where(irrep_ids[:, None] == owners[None, :], block_sizes[None, :], 0), axis=1
    )
    return slot_ids % BLK < limits


def on_device(integrals, amplitudes, block_sizes):
    a_count = integrals.shape[0]
    window = integrals.shape[1]
    per_irrep = window // IRREPS
    c_rows = amplitudes.shape[1]
    own_block = lax.axis_index("cd")
    row_first = lax.axis_index("ab") * a_count
    keep_rows = occupied_slots(block_sizes, lax.axis_index("ab") * c_rows, c_rows)
    keep_cols = occupied_slots(block_sizes, own_block * BLK, BLK)
    keep_mask = keep_rows[:, None] & keep_cols[None, :]
    masked = jnp.where(keep_mask[None], amplitudes, jnp.zeros_like(amplitudes))
    panels = lax.all_gather(masked, "ab", axis=1, tiled=True)
    first_irrep = row_first // per_irrep
    pieces = []
    for second in range(IRREPS):
        source = jnp.bitwise_xor(jnp.bitwise_xor(first_irrep, second), own_block)
        amp_block = lax.dynamic_slice_in_dim(panels, source * BLK, BLK, 1)
        row_block = integrals[:, second * per_irrep : (second + 1) * per_irrep]
        pieces.append(
            jnp.einsum("abcd,pcd->pab", row_block, amp_block, preferred_element_type=jnp.float32)
        )
    partial_sum = jnp.concatenate(pieces, axis=2)
    ladder = lax.psum(partial_sum, "cd")
    mirrored = lax.all_to_all(ladder, "ab", split_axis=2, concat_axis=1, tiled=True)
    return ladder + jnp.transpose(mirrored, (0, 2, 1))


def solution(mesh):
    placed = (P("ab", None, None, "cd"), P(None, "ab", "cd"), P())
    return jax.shard_map(
        on_device, mesh=mesh, in_specs=placed, out_specs=P(None, "ab", None), check_vma=False
    )
```

profile of v0, /device:TPU:0, one launch (start us, length us, event | category | flops | bytes accessed | tf_op | source)
XLA Modules:
  0.0 215.9 jit_solution(4799325225221977902)
XLA Ops:
  6.5 0.0 all-gather.2.cloned.1.call-start
  6.5 0.7 select_reduce_fusion
  7.3 0.7 select_reduce_fusion.1
  8.1 0.1 broadcast_and_fusion
  8.2 1.5 copy_select_fusion
  9.6 0.0 all-gather.2.cloned.1.call-update
  9.7 7.4 %fusion.34 = (bf16[3,24,128,128]{3,2,1,0:T(8,128)(2,1)}, bf16[3,24,128,128]{3,2,1,0:T(8,128)(2,1)}, bf16[3,24,128,128]{3,2,1,0:T(8,128)(2,1)}, bf16[3,24,128,128]{3,2,1,0:T(8,128)(2,1)S(1)}) fusion(bf16[3,96,128,128]{3,2,1,0:T(8,128)(2,1)} %param.3), kind=kLoop, calls=%fused_computation.46 | loop fusion | bytes 18874368 | tf_op jit(solution)/shard_map/slice | solution.py:37
  17.1 148.4 %all-gather.2.cloned.1.call-done = bf16[16,512,128]{2,0,1:T(8,128)(2,1)} async-done(((bf16[16,16,128]{2,0,1:T(8,128)(2,1)}), bf16[16,512,128]{2,0,1:T(8,128)(2,1)}) %all-gather.2.cloned.1.call-update) | async-done | bytes 2097168 | tf_op jit(solution)/shard_map/all_gather | solution.py:31
  165.5 0.0 copy-start.1
  165.5 3.7 %fusion.11 = f32[16,3,24]{2,0,1:T(8,128)S(1)} fusion(bf16[3,24,128,128]{3,2,1,0:T(8,128)(2,1)} %get-tuple-element.7, bf16[16,512,128]{2,0,1:T(8,128)(2,1)} %all-gather.2.cloned.1.call-done, s32[]{:T(128)S(6)} %select_n.76), kind=kOutput, calls=%fused_computation.9 | convolution fusion | flops 37748736 | bytes 2888196 | tf_op jit(solution)/shard_map/abcd,pcd->pab/dot_general | solution.py:39
  169.2 0.0 copy-start
  169.2 0.0 copy-done.1
  169.2 3.0 %fusion.8 = f32[16,3,24]{2,0,1:T(8,128)S(1)} fusion(bf16[3,24,128,128]{3,2,1,0:T(8,128)(2,1)S(1)} %copy-done.1, bf16[16,512,128]{2,0,1:T(8,128)(2,1)} %all-gather.2.cloned.1.call-done, s32[]{:T(128)S(6)} %select_n.75), kind=kOutput, calls=%fused_computation.8 | convolution fusion | flops 37748736 | bytes 2888196 | tf_op jit(solution)/shard_map/abcd,pcd->pab/dot_general | solution.py:39
  172.2 0.0 copy-done
  172.2 2.8 %fusion.14 = f32[16,3,24]{2,0,1:T(8,128)S(1)} fusion(bf16[3,24,128,128]{3,2,1,0:T(8,128)(2,1)S(1)} %copy-done, bf16[16,512,128]{2,0,1:T(8,128)(2,1)} %all-gather.2.cloned.1.call-done, s32[]{:T(128)S(6)} %select_n.77), kind=kOutput, calls=%fused_computation.10 | convolution fusion | flops 37748736 | bytes 2888196 | tf_op jit(solution)/shard_map/abcd,pcd->pab/dot_general | solution.py:39
  175.0 2.8 %fusion.17 = f32[16,3,24]{2,0,1:T(8,128)S(1)} fusion(bf16[3,24,128,128]{3,2,1,0:T(8,128)(2,1)S(1)} %get-tuple-element.8, bf16[16,512,128]{2,0,1:T(8,128)(2,1)} %all-gather.2.cloned.1.call-done, s32[]{:T(128)S(6)} %select_n.78), kind=kOutput, calls=%fused_computation.11 | convolution fusion | flops 37748736 | bytes 2888196 | tf_op jit(solution)/shard_map/abcd,pcd->pab/dot_general | solution.py:39
  177.8 0.1 pad_maximum_fusion
  177.9 13.3 %psum.7 = f32[16,3,96]{2,0,1:T(8,128)S(1)} all-reduce(f32[16,3,96]{2,0,1:T(8,128)S(1)} %pad_maximum_fusion), channel_id=1, replica_groups=mesh['ab'=32,'cd'=4] {'cd'}, use_global_device_ids=true, to_apply=%region_2.3 | all-reduce | flops 4608 | bytes 36864 | tf_op jit(solution)/shard_map/psum | solution.py:42
  191.2 0.1 copy.32
  191.3 0.2 reshape.108
  191.5 15.4 %all_to_all.18 = f32[32,1,144]{2,1,0:T(1,128)S(1)} all-to-all(f32[32,1,144]{2,1,0:T(1,128)S(1)} %reshape.108), channel_id=1, replica_groups=mesh['ab'=32,'cd'=4] {'ab'}, dimensions={0} | all-to-all | bytes 36864 | tf_op jit(solution)/shard_map/all_to_all | solution.py:43
  206.8 0.5 broadcast.182
  207.3 0.7 reduce
  208.1 0.1 reshape.109
  208.3 0.1 all_to_all.16
  208.3 0.1 copy.35
  208.4 0.6 bitcast_add_fusion
  (5 shorter events, 0.1 us)
Async XLA Ops:
  6.5 158.9 %all-gather.2.cloned.1.call-start = ((), (), s32[]{:S(2)}) async-start(), calls=%async_computation.1 | async-start | bytes 2162688 | tf_op jit(solution)/shard_map/all_gather | solution.py:31
  165.5 3.7 %copy-start.1 = (bf16[3,24,128,128]{3,2,1,0:T(8,128)(2,1)S(1)}, bf16[3,24,128,128]{3,2,1,0:T(8,128)(2,1)}, u32[]{:S(2)}) copy-start(bf16[3,24,128,128]{3,2,1,0:T(8,128)(2,1)} %get-tuple-element.5) | copy-start | bytes 7077892
  169.2 3.0 %copy-start = (bf16[3,24,128,128]{3,2,1,0:T(8,128)(2,1)S(1)}, bf16[3,24,128,128]{3,2,1,0:T(8,128)(2,1)}, u32[]{:S(2)}) copy-start(bf16[3,24,128,128]{3,2,1,0:T(8,128)(2,1)} %get-tuple-element.6) | copy-start | bytes 7077892
Sparse Core Ops, SparseCore 0:
  9.8 155.6 all-gather.1
where the time goes:
time: 216 us
  waiting for transfers between devices  148 us (69%)
  blocking collectives  28.6 us (13%)
  between operations  13.5 us (6%)
  matrix products  12.3 us (6%)
  local copies, waits for them, and re-layouts  8.51 us (4%)
  other arithmetic  4.54 us (2%)
    all_gather x1, waiting for transfers between devices, on_device(): panels = lax.all_gather(masked, 'ab', axis=1, tiled=True)  148 us
    all_to_all x1, blocking collectives, on_device(): lax.all_to_all(ladder, 'ab', split_axis=2, concat_axis=1, tiled=True)  15.4 us
    psum x1, blocking collectives, on_device(): ladder = lax.psum(partial_sum, 'cd')  13.3 us
    dot_general x4, matrix products, on_device(): jnp.einsum('abcd,pcd->pab', row_block, amp_block, preferred_element_type=...  12.3 us
    slice x1, local copies, waits for them, and re-layouts, on_device(): row_block = integrals[:, second * per_irrep:(second + 1) * per_irrep]  7.4 us
  transfers between devices with their start and end apart: 1, of which 1 were waited for; matrix products, arithmetic and copies ran while one was open for 3% of the time, Pallas kernels for 0%

commit v1 on v0

--- a/solution.py
+++ b/solution.py
@@ -28,7 +28,9 @@
     keep_cols = occupied_slots(block_sizes, own_block * BLK, BLK)
     keep_mask = keep_rows[:, None] & keep_cols[None, :]
     masked = jnp.where(keep_mask[None], amplitudes, jnp.zeros_like(amplitudes))
-    panels = lax.all_gather(masked, "ab", axis=1, tiled=True)
+    panels = jnp.concatenate(
+        lax.all_to_all(jnp.stack([masked] * lax.axis_size("ab")), "ab", 0, 0), axis=1
+    )
     first_irrep = row_first // per_irrep
     pieces = []
     for second in range(IRREPS):

time: 216 us -> 87.2 us (0.40)
  waiting for transfers between devices: 148 us -> 20.9 us
  between operations: 13.5 us -> 0.13 us
  starting transfers between devices: 0.01 us -> 9.39 us
    all_gather x1 -> x0, waiting for transfers between devices: 148 us -> none  [on_device(): panels = lax.all_gather(masked, 'ab', axis=1, tiled=True)]
    all_to_all x0 -> x1, waiting for transfers between devices: none -> 20.9 us  [on_device(): lax.all_to_all(jnp.stack([masked] * lax.axis_size('ab')), 'ab', 0, 0)]
    all_to_all x0 -> x1, starting transfers between devices: none -> 9.39 us  [on_device(): lax.all_to_all(jnp.stack([masked] * lax.axis_size('ab')), 'ab', 0, 0)]
  transfers between devices with their start and end apart: 1 -> 1, of which waited for: 1 -> 1; matrix products, arithmetic and copies ran while one was open for 3% -> 9% of each run, Pallas kernels for 0% -> 0%
where the time goes in v1:
time: 87.2 us; the launch traced here: 86.7 us
  blocking collectives  29.8 us (34%)
  waiting for transfers between devices  20.9 us (24%)
  matrix products  12.3 us (14%)
  local copies, waits for them, and re-layouts  10.3 us (12%)
  starting transfers between devices  9.39 us (11%)
  other arithmetic  3.91 us (4%)
    all_to_all x1, waiting for transfers between devices, on_device(): lax.all_to_all(jnp.stack([masked] * lax.axis_size('ab')), 'ab', 0, 0)  20.9 us
    all_to_all x1, blocking collectives, on_device(): lax.all_to_all(ladder, 'ab', split_axis=2, concat_axis=1, tiled=True)  15.3 us
    psum x1, blocking collectives, on_device(): ladder = lax.psum(partial_sum, 'cd')  14.5 us
    dot_general x4, matrix products, on_device(): jnp.einsum('abcd,pcd->pab', row_block, amp_block, preferred_element_type=...  12.3 us
    all_to_all x1, starting transfers between devices, on_device(): lax.all_to_all(jnp.stack([masked] * lax.axis_size('ab')), 'ab', 0, 0)  9.39 us
    slice x1, local copies, waits for them, and re-layouts, on_device(): row_block = integrals[:, second * per_irrep:(second + 1) * per_irrep]  7.4 us
    another operation x1, local copies, waits for them, and re-layouts, on_device(): jnp.stack([masked] * lax.axis_size('ab'))  1.79 us
  transfers between devices with their start and end apart: 1, of which 1 were waited for; matrix products, arithmetic and copies ran while one was open for 9% of the time, Pallas kernels for 0%

profile of v1, /device:TPU:0, one launch (start us, length us, event | category | flops | bytes accessed | tf_op | source)
XLA Modules:
  0.0 86.7 jit_solution(7791773805467734397)
XLA Ops:
  0.0 0.7 select_reduce_fusion
  0.8 0.7 select_reduce_fusion.1
  1.5 0.1 broadcast_and_fusion
  1.6 0.8 broadcast_select_fusion
  2.5 1.8 %stack.2 = bf16[32,16,16,128]{3,1,2,0:T(8,128)(2,1)} broadcast(bf16[16,16,128]{2,0,1:T(8,128)(2,1)S(1)} %copy.27), dimensions={1,2,3} | broadcast | bytes 2162688 | tf_op jit(solution)/shard_map/stack | solution.py:32
  4.3 9.4 %all-to-all-start = ((bf16[32,16,16,128]{3,1,2,0:T(8,128)(2,1)}), bf16[32,16,16,128]{3,1,2,0:T(8,128)(2,1)}, u32[]{:S(2)}, u32[]{:S(2)}) async-start(bf16[32,16,16,128]{3,1,2,0:T(8,128)(2,1)} %stack.2), calls=%async_computation | async-start | bytes 4194304 | tf_op jit(solution)/shard_map/all_to_all | solution.py:32
  13.7 7.4 %fusion.34 = (bf16[3,24,128,128]{3,2,1,0:T(8,128)(2,1)}, bf16[3,24,128,128]{3,2,1,0:T(8,128)(2,1)}, bf16[3,24,128,128]{3,2,1,0:T(8,128)(2,1)}, bf16[3,24,128,128]{3,2,1,0:T(8,128)(2,1)S(1)}) fusion(bf16[3,96,128,128]{3,2,1,0:T(8,128)(2,1)} %param.3), kind=kLoop, calls=%fused_computation.46 | loop fusion | bytes 18874368 | tf_op jit(solution)/shard_map/slice | solution.py:39
  21.1 20.9 %all-to-all-done = bf16[32,16,16,128]{3,1,2,0:T(8,128)(2,1)} async-done(((bf16[32,16,16,128]{3,1,2,0:T(8,128)(2,1)}), bf16[32,16,16,128]{3,1,2,0:T(8,128)(2,1)}, u32[]{:S(2)}, u32[]{:S(2)}) %all-to-all-start) | async-done | bytes 2097184 | tf_op jit(solution)/shard_map/all_to_all | solution.py:32
  42.0 0.0 copy-start.1
  42.0 3.7 %fusion.11 = f32[16,3,24]{2,0,1:T(8,128)S(1)} fusion(bf16[3,24,128,128]{3,2,1,0:T(8,128)(2,1)} %get-tuple-element.7, bf16[16,512,128]{2,0,1:T(8,128)(2,1)} %bitcast.1, s32[]{:T(128)S(6)} %select_n.76), kind=kOutput, calls=%fused_computation.9 | convolution fusion | flops 37748736 | bytes 2888196 | tf_op jit(solution)/shard_map/abcd,pcd->pab/dot_general | solution.py:41
  45.7 0.0 copy-start
  45.7 0.0 copy-done.1
  45.7 3.0 %fusion.8 = f32[16,3,24]{2,0,1:T(8,128)S(1)} fusion(bf16[3,24,128,128]{3,2,1,0:T(8,128)(2,1)S(1)} %copy-done.1, bf16[16,512,128]{2,0,1:T(8,128)(2,1)} %bitcast.1, s32[]{:T(128)S(6)} %select_n.75), kind=kOutput, calls=%fused_computation.8 | convolution fusion | flops 37748736 | bytes 2888196 | tf_op jit(solution)/shard_map/abcd,pcd->pab/dot_general | solution.py:41
  48.7 0.0 copy-done
  48.7 2.8 %fusion.14 = f32[16,3,24]{2,0,1:T(8,128)S(1)} fusion(bf16[3,24,128,128]{3,2,1,0:T(8,128)(2,1)S(1)} %copy-done, bf16[16,512,128]{2,0,1:T(8,128)(2,1)} %bitcast.1, s32[]{:T(128)S(6)} %select_n.77), kind=kOutput, calls=%fused_computation.10 | convolution fusion | flops 37748736 | bytes 2888196 | tf_op jit(solution)/shard_map/abcd,pcd->pab/dot_general | solution.py:41
  51.6 2.8 %fusion.17 = f32[16,3,24]{2,0,1:T(8,128)S(1)} fusion(bf16[3,24,128,128]{3,2,1,0:T(8,128)(2,1)S(1)} %get-tuple-element.8, bf16[16,512,128]{2,0,1:T(8,128)(2,1)} %bitcast.1, s32[]{:T(128)S(6)} %select_n.78), kind=kOutput, calls=%fused_computation.11 | convolution fusion | flops 37748736 | bytes 2888196 | tf_op jit(solution)/shard_map/abcd,pcd->pab/dot_general | solution.py:41
  54.3 0.1 pad_maximum_fusion
  54.4 14.5 %psum.7 = f32[16,3,96]{2,0,1:T(8,128)S(1)} all-reduce(f32[16,3,96]{2,0,1:T(8,128)S(1)} %pad_maximum_fusion), channel_id=1, replica_groups=mesh['ab'=32,'cd'=4] {'cd'}, use_global_device_ids=true, to_apply=%region_2.3 | all-reduce | flops 4608 | bytes 36864 | tf_op jit(solution)/shard_map/psum | solution.py:44
  68.9 0.1 copy.32
  69.1 0.2 reshape.118
  69.2 15.3 %all_to_all.23 = f32[32,1,144]{2,1,0:T(1,128)S(1)} all-to-all(f32[32,1,144]{2,1,0:T(1,128)S(1)} %reshape.118), channel_id=1, replica_groups=mesh['ab'=32,'cd'=4] {'ab'}, dimensions={0} | all-to-all | bytes 36864 | tf_op jit(solution)/shard_map/all_to_all | solution.py:45
  84.5 0.5 broadcast.184
  85.0 0.7 reduce
  85.8 0.1 reshape.119
  86.0 0.1 all_to_all.20
  86.0 0.1 copy.35
  86.1 0.6 bitcast_add_fusion
  (6 shorter events, 0.1 us)
Async XLA Ops:
  4.3 37.7 %all-to-all-start = ((bf16[32,16,16,128]{3,1,2,0:T(8,128)(2,1)}), bf16[32,16,16,128]{3,1,2,0:T(8,128)(2,1)}, u32[]{:S(2)}, u32[]{:S(2)}) async-start(bf16[32,16,16,128]{3,1,2,0:T(8,128)(2,1)} %stack.2), calls=%async_computation | async-start | bytes 4194304 | tf_op jit(solution)/shard_map/all_to_all | solution.py:32
  42.0 3.7 %copy-start.1 = (bf16[3,24,128,128]{3,2,1,0:T(8,128)(2,1)S(1)}, bf16[3,24,128,128]{3,2,1,0:T(8,128)(2,1)}, u32[]{:S(2)}) copy-start(bf16[3,24,128,128]{3,2,1,0:T(8,128)(2,1)} %get-tuple-element.5) | copy-start | bytes 7077892
  45.7 3.0 %copy-start = (bf16[3,24,128,128]{3,2,1,0:T(8,128)(2,1)S(1)}, bf16[3,24,128,128]{3,2,1,0:T(8,128)(2,1)}, u32[]{:S(2)}) copy-start(bf16[3,24,128,128]{3,2,1,0:T(8,128)(2,1)} %get-tuple-element.6) | copy-start | bytes 7077892

commit v2 on v0

--- a/solution.py
+++ b/solution.py
@@ -39,7 +39,7 @@
             jnp.einsum("abcd,pcd->pab", row_block, amp_block, preferred_element_type=jnp.float32)
         )
     partial_sum = jnp.concatenate(pieces, axis=2)
-    ladder = lax.psum(partial_sum, "cd")
+    ladder = jnp.sum(lax.all_gather(partial_sum, "cd"), axis=0)
     mirrored = lax.all_to_all(ladder, "ab", split_axis=2, concat_axis=1, tiled=True)
     return ladder + jnp.transpose(mirrored, (0, 2, 1))
 

time: 216 us -> 210 us (0.972)
  blocking collectives: 28.6 us -> 22.2 us
    psum x1 -> x0, blocking collectives: 13.3 us -> none  [on_device(): ladder = lax.psum(partial_sum, 'cd')]
    all_gather x0 -> x1, blocking collectives: none -> 6.84 us  [on_device(): ladder = jnp.sum(lax.all_gather(partial_sum, 'cd'), axis=0)]
  transfers between devices with their start and end apart: 1 -> 1, of which waited for: 1 -> 1; matrix products, arithmetic and copies ran while one was open for 3% -> 4% of each run, Pallas kernels for 0% -> 0%
where the time goes in v2:
time: 210 us; the launch traced here: 209 us
  waiting for transfers between devices  148 us (70%)
  blocking collectives  22.2 us (11%)
  between operations  13.5 us (6%)
  matrix products  12.3 us (6%)
  local copies, waits for them, and re-layouts  8.51 us (4%)
  other arithmetic  4.56 us (2%)
    all_gather x1, waiting for transfers between devices, on_device(): panels = lax.all_gather(masked, 'ab', axis=1, tiled=True)  148 us
    all_to_all x1, blocking collectives, on_device(): lax.all_to_all(ladder, 'ab', split_axis=2, concat_axis=1, tiled=True)  15.4 us
    dot_general x4, matrix products, on_device(): jnp.einsum('abcd,pcd->pab', row_block, amp_block, preferred_element_type=...  12.3 us
    slice x1, local copies, waits for them, and re-layouts, on_device(): row_block = integrals[:, second * per_irrep:(second + 1) * per_irrep]  7.4 us
    all_gather x1, blocking collectives, on_device(): ladder = jnp.sum(lax.all_gather(partial_sum, 'cd'), axis=0)  6.84 us
  transfers between devices with their start and end apart: 1, of which 1 were waited for; matrix products, arithmetic and copies ran while one was open for 4% of the time, Pallas kernels for 0%

profile of v2, /device:TPU:0, one launch (start us, length us, event | category | flops | bytes accessed | tf_op | source)
XLA Modules:
  0.0 209.5 jit_solution(13628820816592851074)
XLA Ops:
  6.5 0.0 all-gather.3.cloned.1.call-start
  6.5 0.7 select_reduce_fusion
  7.3 0.7 select_reduce_fusion.1
  8.1 0.1 broadcast_and_fusion
  8.2 1.5 copy_select_fusion
  9.6 0.0 all-gather.3.cloned.1.call-update
  9.7 7.4 %fusion.34 = (bf16[3,24,128,128]{3,2,1,0:T(8,128)(2,1)}, bf16[3,24,128,128]{3,2,1,0:T(8,128)(2,1)}, bf16[3,24,128,128]{3,2,1,0:T(8,128)(2,1)}, bf16[3,24,128,128]{3,2,1,0:T(8,128)(2,1)S(1)}) fusion(bf16[3,96,128,128]{3,2,1,0:T(8,128)(2,1)} %param.3), kind=kLoop, calls=%fused_computation.46 | loop fusion | bytes 18874368 | tf_op jit(solution)/shard_map/slice | solution.py:37
  17.1 148.4 %all-gather.3.cloned.1.call-done = bf16[16,512,128]{2,0,1:T(8,128)(2,1)} async-done(((bf16[16,16,128]{2,0,1:T(8,128)(2,1)}), bf16[16,512,128]{2,0,1:T(8,128)(2,1)}) %all-gather.3.cloned.1.call-update) | async-done | bytes 2097168 | tf_op jit(solution)/shard_map/all_gather | solution.py:31
  165.5 0.0 copy-start.1
  165.5 3.7 %fusion.11 = f32[16,3,24]{2,0,1:T(8,128)S(1)} fusion(bf16[3,24,128,128]{3,2,1,0:T(8,128)(2,1)} %get-tuple-element.7, bf16[16,512,128]{2,0,1:T(8,128)(2,1)} %all-gather.3.cloned.1.call-done, s32[]{:T(128)S(6)} %select_n.76), kind=kOutput, calls=%fused_computation.9 | convolution fusion | flops 37748736 | bytes 2888196 | tf_op jit(solution)/shard_map/abcd,pcd->pab/dot_general | solution.py:39
  169.2 0.0 copy-start
  169.2 0.0 copy-done.1
  169.2 3.0 %fusion.8 = f32[16,3,24]{2,0,1:T(8,128)S(1)} fusion(bf16[3,24,128,128]{3,2,1,0:T(8,128)(2,1)S(1)} %copy-done.1, bf16[16,512,128]{2,0,1:T(8,128)(2,1)} %all-gather.3.cloned.1.call-done, s32[]{:T(128)S(6)} %select_n.75), kind=kOutput, calls=%fused_computation.8 | convolution fusion | flops 37748736 | bytes 2888196 | tf_op jit(solution)/shard_map/abcd,pcd->pab/dot_general | solution.py:39
  172.2 0.0 copy-done
  172.2 2.8 %fusion.14 = f32[16,3,24]{2,0,1:T(8,128)S(1)} fusion(bf16[3,24,128,128]{3,2,1,0:T(8,128)(2,1)S(1)} %copy-done, bf16[16,512,128]{2,0,1:T(8,128)(2,1)} %all-gather.3.cloned.1.call-done, s32[]{:T(128)S(6)} %select_n.77), kind=kOutput, calls=%fused_computation.10 | convolution fusion | flops 37748736 | bytes 2888196 | tf_op jit(solution)/shard_map/abcd,pcd->pab/dot_general | solution.py:39
  175.0 2.8 %fusion.17 = f32[16,3,24]{2,0,1:T(8,128)S(1)} fusion(bf16[3,24,128,128]{3,2,1,0:T(8,128)(2,1)S(1)} %get-tuple-element.8, bf16[16,512,128]{2,0,1:T(8,128)(2,1)} %all-gather.3.cloned.1.call-done, s32[]{:T(128)S(6)} %select_n.78), kind=kOutput, calls=%fused_computation.11 | convolution fusion | flops 37748736 | bytes 2888196 | tf_op jit(solution)/shard_map/abcd,pcd->pab/dot_general | solution.py:39
  177.8 0.1 pad_maximum_fusion
  177.9 6.8 %all-gather = f32[64,3,96]{2,0,1:T(8,128)S(1)} all-gather(f32[16,3,96]{2,0,1:T(8,128)S(1)} %pad_maximum_fusion), channel_id=2, replica_groups=mesh['ab'=32,'cd'=4] {'cd'}, dimensions={0}, use_global_device_ids=true | all-gather | bytes 92160 | tf_op jit(solution)/shard_map/all_gather | solution.py:42
  184.8 0.1 copy.31
  184.9 0.2 reshape.109
  185.0 15.4 %all_to_all.18 = f32[32,1,144]{2,1,0:T(1,128)S(1)} all-to-all(f32[32,1,144]{2,1,0:T(1,128)S(1)} %reshape.109), channel_id=1, replica_groups=mesh['ab'=32,'cd'=4] {'ab'}, dimensions={0} | all-to-all | bytes 36864 | tf_op jit(solution)/shard_map/all_to_all | solution.py:43
  200.4 0.5 broadcast.182
  200.9 0.7 reduce
  201.7 0.1 reshape.110
  201.8 0.1 all_to_all.16
  201.9 0.1 copy.34
  202.0 0.6 bitcast_add_fusion
  (6 shorter events, 0.1 us)
Async XLA Ops:
  6.5 158.9 %all-gather.3.cloned.1.call-start = ((), (), s32[]{:S(2)}) async-start(), calls=%async_computation.1 | async-start | bytes 2162688 | tf_op jit(solution)/shard_map/all_gather | solution.py:31
  165.5 3.7 %copy-start.1 = (bf16[3,24,128,128]{3,2,1,0:T(8,128)(2,1)S(1)}, bf16[3,24,128,128]{3,2,1,0:T(8,128)(2,1)}, u32[]{:S(2)}) copy-start(bf16[3,24,128,128]{3,2,1,0:T(8,128)(2,1)} %get-tuple-element.5) | copy-start | bytes 7077892
  169.2 3.0 %copy-start = (bf16[3,24,128,128]{3,2,1,0:T(8,128)(2,1)S(1)}, bf16[3,24,128,128]{3,2,1,0:T(8,128)(2,1)}, u32[]{:S(2)}) copy-start(bf16[3,24,128,128]{3,2,1,0:T(8,128)(2,1)} %get-tuple-element.6) | copy-start | bytes 7077892
Sparse Core Ops, SparseCore 0:
  9.8 155.6 all-gather.2
